TPU v7x, 32 devices: a whole 2x2x4 slice. The times are simulated.
32 devices in a mesh: seq: 16 (over z, y, x), head: 2 (over core).
Axes of the slice: x: 2, y: 2, z: 4, core: 2. Of those that a mesh axis runs over, the one named last changes fastest.
Arguments:
- q_lin: bfloat16 [4096, 512], P('seq', 'head'), may hold values from -6 to 6
- k_lin: bfloat16 [4096, 512], P('seq', 'head'), may hold values from -6 to 6
- v_lin: bfloat16 [4096, 512], P('seq', 'head'), may hold values from -6 to 6
- log_decay: float32 [4, 4096], P('head', 'seq'), may hold values from -0.4 to 0, as said below
- q_soft: bfloat16 [4096, 512], P('seq', 'head'), may hold values from -12 to 12
- k_soft: bfloat16 [4096, 512], P('seq', 'head'), may hold values from -6 to 6
- v_soft: bfloat16 [4096, 512], P('seq', 'head'), may hold values from -6 to 6
- wo_lin: bfloat16 [512, 4096], P('head'), may hold values from -0.375 to 0.375
- wo_soft: bfloat16 [512, 4096], P('head'), may hold values from -0.375 to 0.375
Outputs:
- lin_mixed: bfloat16 [4096, 4096], P('seq', 'head')
- soft_mixed: bfloat16 [4096, 4096], P('seq', 'head')
Inputs may be any that keep to these rules, and one draw needn't show every extreme that they name: `log_decay`: log decays are never positive.
All inputs are finite; a program needn't handle non-finite values.
Results may differ from a plain program's by a relative error of at most 0.012.
Values may be sent and summed in bfloat16 or wider, within the bound.
A program may use at most 64 MiB of HBM per device.

v0:
```python
import math
import jax
import jax.numpy as jnp
from jax import lax
from jax.sharding import PartitionSpec as P

HIGHEST = lax.Precision.HIGHEST
NEG_BIG = -1e30


def prefix(shard, axis, combine, identity):
    size, here = (lax.axis_size(axis), lax.axis_index(axis))
    everything = jax.tree.map(
        lambda part, kind: lax.all_gather(part.astype(kind), axis),
        shard,
        (jnp.bfloat16, jnp.bfloat16),
    )
    start = jax.tree.map(
        lambda part, zero: jnp.broadcast_to(jnp.asarray(zero, part.dtype), part.shape),
        shard,
        identity,
    )

    def turn(k, before):
        reached = k < here
        new = combine(
            before, jax.tree.map(lambda part, own: part[k].astype(own.dtype), everything, shard)
        )
        return jax.tree.map(lambda a, b: jnp.where(reached, a, b), new, before)

    return lax.fori_loop(0, size, turn, start)


def second_half(device):
    return 2 * device + 1


def absorb(state, query_half, key_block, value_block, allowed, factor):
    row_top, row_sum, weighted = state
    scores = (
        jnp.einsum("qhd,khd->hqk", query_half, key_block, preferred_element_type=jnp.float32)
        * factor
    )
    if allowed is not None:
        scores = jnp.where(allowed[None], scores, -jnp.inf)
    new_top = jnp.maximum(row_top, jnp.max(scores, axis=-1))
    shrink = jnp.exp(row_top - new_top)
    weights = jnp.exp(scores - new_top[:, :, None])
    row_sum = row_sum * shrink + jnp.sum(weights, axis=-1)
    weighted = weighted * shrink.T[:, :, None] + jnp.einsum(
        "hqk,khd->qhd",
        weights.astype(jnp.bfloat16),
        value_block,
        preferred_element_type=jnp.float32,
    )
    return (new_top, row_sum, weighted)


def lightning_heads(q_lin, k_lin, v_lin, log_decay):
    row_count = q_lin.shape[0]
    head_count = log_decay.shape[0]
    head_width = q_lin.shape[1] // head_count
    query_plain = q_lin.reshape(row_count, head_count, head_width)
    key_plain = k_lin.reshape(row_count, head_count, head_width)
    queries = query_plain.astype(jnp.float32)
    key_rows = key_plain.astype(jnp.float32)
    values = v_lin.astype(jnp.float32).reshape(row_count, head_count, head_width)
    cumulative = jnp.cumsum(log_decay, axis=1)
    lower = jnp.arange(row_count)[:, None] >= jnp.arange(row_count)[None, :]
    decay_gap = jnp.where(lower[None], cumulative[:, :, None] - cumulative[:, None, :], -jnp.inf)
    scores = jnp.einsum(
        "thd,shd->hts", query_plain, key_plain, preferred_element_type=jnp.float32
    ) * jnp.exp(decay_gap)
    inside = jnp.einsum("hts,shd->thd", scores, values, precision=HIGHEST)
    closing = jnp.exp(cumulative[:, -1:] - cumulative)
    own_state = jnp.einsum(
        "shd,she->hde", key_rows * closing.T[:, :, None], values, precision=HIGHEST
    )
    own_decay = cumulative[:, -1]

    def combine(earlier, later):
        return (jnp.exp(later[1])[:, None, None] * earlier[0] + later[0], earlier[1] + later[1])

    identity = (jnp.zeros_like(own_state), jnp.zeros_like(own_decay))
    carried, _ = prefix((own_state, own_decay), "seq", combine, identity)
    from_before = (
        jnp.einsum("thd,hde->the", queries, carried, precision=HIGHEST)
        * jnp.exp(cumulative).T[:, :, None]
    )
    raw = inside + from_before
    factor = lax.rsqrt(jnp.mean(raw * raw, axis=-1, keepdims=True) + 1e-06)
    return (raw * factor).astype(jnp.bfloat16).reshape(row_count, head_count * head_width)


def softmax_heads(q_soft, k_soft, v_soft, head_width):
    row_count = q_soft.shape[0]
    half_rows = row_count // 2
    head_count = q_soft.shape[1] // head_width
    own_index = lax.axis_index("seq")
    factor = 1.0 / math.sqrt(head_width)
    shaped = q_soft.reshape(2, half_rows, head_count, head_width)
    query_ids = (2 * own_index, second_half(own_index))
    triangle = jnp.arange(half_rows)[:, None] >= jnp.arange(half_rows)[None, :]

    def block_pass(state, side, key_block, value_block, key_id):

        def full_block(inner_state):
            return absorb(inner_state, shaped[side], key_block, value_block, None, factor)

        def diagonal_block(inner_state):
            return absorb(inner_state, shaped[side], key_block, value_block, triangle, factor)

        def skipped(inner_state):
            return inner_state

        def not_below(inner_state):
            return lax.cond(key_id == query_ids[side], diagonal_block, skipped, inner_state)

        return lax.cond(key_id < query_ids[side], full_block, not_below, state)

    start_state = tuple(
        (
            (
                jnp.full((head_count, half_rows), NEG_BIG, jnp.float32),
                jnp.zeros((head_count, half_rows), jnp.float32),
                jnp.zeros((half_rows, head_count, head_width), jnp.float32),
            )
            for side in range(2)
        )
    )
    carry = start_state
    key_piece = lax.all_gather(k_soft, "seq", axis=0, tiled=True)
    value_piece = lax.all_gather(v_soft, "seq", axis=0, tiled=True)
    piece_rows = key_piece.shape[0]
    blocks = piece_rows // half_rows
    key_blocks = key_piece.reshape(blocks, half_rows, head_count, head_width)
    value_blocks = value_piece.reshape(blocks, half_rows, head_count, head_width)
    firsts = half_rows * jnp.arange(blocks, dtype=jnp.int32)

    def inner(state, block_item):
        key_block, value_block, first = block_item
        key_id = first // half_rows
        return (
            tuple(
                (block_pass(state[side], side, key_block, value_block, key_id) for side in range(2))
            ),
            None,
        )

    carry, _ = lax.scan(inner, carry, (key_blocks, value_blocks, firsts))
    halves = [
        (carry[side][2] / carry[side][1].T[:, :, None])
        .astype(jnp.bfloat16)
        .reshape(half_rows, head_count * head_width)
        for side in range(2)
    ]
    return jnp.concatenate(halves, axis=0)


def local(q_lin, k_lin, v_lin, log_decay, q_soft, k_soft, v_soft, wo_lin, wo_soft):
    head_width = q_lin.shape[1] // log_decay.shape[0]
    lin_out = lightning_heads(q_lin, k_lin, v_lin, log_decay)
    soft_out = softmax_heads(q_soft, k_soft, v_soft, head_width)
    lin_term = jnp.dot(lin_out, wo_lin, preferred_element_type=jnp.float32)
    soft_term = jnp.dot(soft_out, wo_soft, preferred_element_type=jnp.float32)
    lin_sum, soft_sum = (
        lax.psum_scatter(
            lin_term.astype(jnp.bfloat16).astype(jnp.float32).astype(jnp.bfloat16),
            "head",
            scatter_dimension=1,
            tiled=True,
        ).astype(jnp.float32),
        lax.psum_scatter(
            soft_term.astype(jnp.bfloat16).astype(jnp.float32).astype(jnp.bfloat16),
            "head",
            scatter_dimension=1,
            tiled=True,
        ).astype(jnp.float32),
    )
    return (lin_sum.astype(jnp.bfloat16), soft_sum.astype(jnp.bfloat16))


def solution(mesh):
    in_specs = (
        P("seq", "head"),
        P("seq", "head"),
        P("seq", "head"),
        P("head", "seq"),
        P("seq", "head"),
        P("seq", "head"),
        P("seq", "head"),
        P("head", None),
        P("head", None),
    )
    out_specs = (P("seq", "head"), P("seq", "head"))
    return jax.shard_map(local, mesh=mesh, in_specs=in_specs, out_specs=out_specs, check_vma=False)
```

profile of v0, /device:TPU:0, one launch (start us, length us, event | category | flops | bytes accessed | tf_op | source)
XLA Modules:
  0.0 389.1 jit_solution(17133437121583700277)
XLA Ops:
  9.3 1.0 copy.69
  10.4 1.8 convolution_convert_fusion.2
  13.8 1.2 dynamic-slice
  15.9 43.7 %all-reduce = bf16[32]{0:T(256)(128)(2,1)S(1)} all-reduce(bf16[32]{0:T(256)(128)(2,1)S(1)} %dynamic-update-slice), channel_id=2, replica_groups=mesh['seq'=16,'head'=2] {'seq'}, use_global_device_ids=true, to_apply=%add | all-reduce | flops 32 | bytes 128
  60.7 1.1 convolution_multiply_fusion.4
  61.8 8.6 %all-gather.10.cloned.1.call-done = bf16[32,128,128]{2,1,0:T(8,128)(2,1)} async-done(((bf16[2,128,128]{2,1,0:T(8,128)(2,1)}), bf16[32,128,128]{2,1,0:T(8,128)(2,1)}) %all-gather.10.cloned.1.call-update) | async-done | bytes 1048592 | tf_op jit(solution)/shard_map/all_gather | solution.py:14
  70.5 15.6 %while.39 = (s32[]{:T(128)}, f32[2,128,128]{2,1,0:T(8,128)S(1)}, s32[]{:T(128)}, bf16[16,2]{1,0:T(8,128)(2,1)S(1)}, bf16[16,2,128,128]{3,2,1,0:T(8,128)(2,1)}, /*index=5*/s32[]{:T(128)}, s32[]{:T(128)}) while((s32[]{:T(128)}, f32[2,128,128]{2,1,0:T(8,128)S(1)}, s32[]{:T(128)}, bf16[16,2]{1,0:T(8,128)(2,1)S(1)}, ...), condition=%wide.region_3.4_spmd.clone, body=%wide.region_2.3_spmd.clone.sunk | while | flops 163846 | bytes 327813 | solution.py:31
  86.9 2.1 convolution_convert_fusion.1
  89.1 43.7 %all-gather.6.cloned.1.call-done = bf16[4096,256]{1,0:T(8,128)(2,1)} async-done(((bf16[256,256]{1,0:T(8,128)(2,1)}), bf16[4096,256]{1,0:T(8,128)(2,1)}) %all-gather.6.cloned.1.call-update) | async-done | bytes 2097168 | tf_op jit(solution)/shard_map/all_gather | solution.py:132
  132.8 4.0 %reshape.143 = bf16[32,128,2,128]{3,2,1,0:T(2,128)(2,1)} reshape(bf16[4096,256]{1,0:T(8,128)(2,1)} %all-gather.6.cloned.1.call-done) | data formatting | bytes 4194304 | tf_op jit(solution)/shard_map/reshape | solution.py:136
  136.8 58.2 %all-gather.8.cloned.1.call-done = bf16[4096,256]{1,0:T(8,128)(2,1)} async-done(((bf16[256,256]{1,0:T(8,128)(2,1)}), bf16[4096,256]{1,0:T(8,128)(2,1)}) %all-gather.8.cloned.1.call-update) | async-done | bytes 2097168 | tf_op jit(solution)/shard_map/all_gather | solution.py:133
  195.0 4.0 %reshape.144 = bf16[32,128,2,128]{3,2,1,0:T(2,128)(2,1)} reshape(bf16[4096,256]{1,0:T(8,128)(2,1)} %all-gather.8.cloned.1.call-done) | data formatting | bytes 4194304 | tf_op jit(solution)/shard_map/reshape | solution.py:137
  199.0 141.2 %while.38 = (s32[]{:T(128)}, f32[2,128]{1,0:T(2,128)S(1)}, f32[2,128]{1,0:T(2,128)S(1)}, f32[128,2,128]{2,0,1:T(8,128)S(1)}, f32[2,128]{1,0:T(2,128)S(1)}, /*ind...) while((s32[]{:T(128)}, f32[2,128]{1,0:T(2,128)S(1)}, ...), condition=%wide.region_23.24_spmd.clone.clone, body=%wide.region_6.23_spmd.clone.clone.sunk | while | flops 34162200 | bytes 2311003 | solution.py:150
  202.3 1.0 constant_dynamic-slice_fusion.3
  207.7 1.0 constant_dynamic-slice_fusion.3
  212.6 1.0 constant_dynamic-slice_fusion.3
  216.9 1.0 constant_dynamic-slice_fusion.3
  221.3 1.0 constant_dynamic-slice_fusion.3
  225.7 1.0 constant_dynamic-slice_fusion.3
  230.0 1.0 constant_dynamic-slice_fusion.3
  234.4 1.0 constant_dynamic-slice_fusion.3
  238.7 1.0 constant_dynamic-slice_fusion.3
  243.1 1.0 constant_dynamic-slice_fusion.3
  247.5 1.0 constant_dynamic-slice_fusion.3
  251.8 1.0 constant_dynamic-slice_fusion.3
  256.2 1.0 constant_dynamic-slice_fusion.3
  260.5 1.0 constant_dynamic-slice_fusion.3
  264.9 1.0 constant_dynamic-slice_fusion.3
  269.3 1.0 constant_dynamic-slice_fusion.3
  273.6 1.0 constant_dynamic-slice_fusion.3
  340.4 3.6 convolution_convert_fusion
  344.1 38.5 %reduce-scatter.5.cloned.1.call-done = bf16[256,2048]{1,0:T(8,128)(2,1)} async-done(((bf16[256,4096]{1,0:T(8,128)(2,1)}), bf16[256,2048]{1,0:T(8,128)(2,1)}) %reduce-scatter.5.cloned.1.call-update) | async-done | bytes 1048592 | tf_op jit(solution)/shard_map/reduce_scatter | solution.py:173
  (369 shorter events, 63.6 us)
Async XLA Ops:
  7.2 79.8 %copy-start = (bf16[256,4096]{1,0:T(8,128)(2,1)S(1)}, bf16[256,4096]{1,0:T(8,128)(2,1)}, u32[]{:S(2)}) copy-start(bf16[256,4096]{1,0:T(8,128)(2,1)} %param.28) | copy-start | bytes 6291460
  7.2 63.3 %all-gather.10.cloned.1.call-start = ((), (), s32[]{:S(2)}) async-start(), calls=%async_computation.6 | async-start | bytes 1114112 | tf_op jit(solution)/shard_map/all_gather | solution.py:14
  10.3 75.7 %copy-start.2 = (bf16[256,256]{1,0:T(8,128)(2,1)S(1)}, bf16[256,256]{1,0:T(8,128)(2,1)}, u32[]{:S(2)}) copy-start(bf16[256,256]{1,0:T(8,128)(2,1)} %param.21) | copy-start | bytes 393220
  12.2 120.6 %all-gather.6.cloned.1.call-start = ((), (), s32[]{:S(2)}) async-start(), calls=%async_computation.3 | async-start | bytes 2228224 | tf_op jit(solution)/shard_map/all_gather | solution.py:132
  13.0 73.4 %copy-start.1 = (bf16[256,256]{1,0:T(8,128)(2,1)S(1)}, bf16[256,256]{1,0:T(8,128)(2,1)}, u32[]{:S(2)}) copy-start(bf16[256,256]{1,0:T(8,128)(2,1)} %param.23) | copy-start | bytes 393220
  13.0 182.0 %all-gather.8.cloned.1.call-start = ((), (), s32[]{:S(2)}) async-start(), calls=%async_computation.4 | async-start | bytes 2228224 | tf_op jit(solution)/shard_map/all_gather | solution.py:133
  13.7 330.4 %reduce-scatter.3.cloned.1.call-start = ((), (), s32[]{:S(2)}) async-start(), calls=%async_computation.2 | async-start | bytes 3145728 | tf_op jit(solution)/shard_map/reduce_scatter | solution.py:167
  89.0 293.5 %reduce-scatter.5.cloned.1.call-start = ((), (), s32[]{:S(2)}) async-start(), calls=%async_computation.5 | async-start | bytes 3145728 | tf_op jit(solution)/shard_map/reduce_scatter | solution.py:173
Sparse Core Ops, SparseCore 0:
  12.3 58.0 all-gather.9
  73.2 59.5 all-gather.5
  135.6 59.3 all-gather.7
  197.6 8.2 reduce-scatter.2
  344.2 38.3 reduce-scatter.4
where the time goes:
time: 393 us; the launch traced here: 389 us
  waiting for transfers between devices  150 us (38%)
  loops' own time  89.1 us (23%)
  local copies, waits for them, and re-layouts  63.5 us (16%)
  blocking collectives  43.7 us (11%)
  other arithmetic  16.9 us (4%)
  between operations  14.6 us (4%)
  matrix products  10.7 us (3%)
    another operation x1, loops' own time, softmax_heads(): carry, _ = lax.scan(inner, carry, (key_blocks, value_blocks, firsts))  85.6 us
    all_gather x1, waiting for transfers between devices, softmax_heads(): value_piece = lax.all_gather(v_soft, 'seq', axis=0, tiled=True)  58.2 us
    dynamic_slice x128, local copies, waits for them, and re-layouts, softmax_heads(): carry, _ = lax.scan(inner, carry, (key_blocks, value_blocks, firsts))  50.6 us
    all_gather x1, waiting for transfers between devices, softmax_heads(): key_piece = lax.all_gather(k_soft, 'seq', axis=0, tiled=True)  43.7 us
    unnamed x1, blocking collectives  43.7 us
    reduce_scatter x1, waiting for transfers between devices, local(): lax.psum_scatter(soft_term.astype(jnp.bfloat16).astype(jnp.float32).astyp...  38.5 us
    select_n x16, other arithmetic, turn(): return jax.tree.map(lambda a, b: jnp.where(reached, a, b), new, before)  14.9 us
    all_gather x1, waiting for transfers between devices, prefix(): lax.all_gather(part.astype(kind), axis)  8.65 us
  transfers between devices with their start and end apart: 5, of which 4 were waited for; matrix products, arithmetic and copies ran while one was open for 22% of the time, Pallas kernels for 0%

commit v1 on v0

--- a/solution.py
+++ b/solution.py
@@ -129,8 +129,11 @@
         )
     )
     carry = start_state
-    key_piece = lax.all_gather(k_soft, "seq", axis=0, tiled=True)
-    value_piece = lax.all_gather(v_soft, "seq", axis=0, tiled=True)
+    key_piece, value_piece = jnp.split(
+        lax.all_gather(jnp.concatenate([k_soft, v_soft], axis=1), "seq", axis=0, tiled=True),
+        [k_soft.shape[1]],
+        axis=1,
+    )
     piece_rows = key_piece.shape[0]
     blocks = piece_rows // half_rows
     key_blocks = key_piece.reshape(blocks, half_rows, head_count, head_width)

time: 393 us -> 355 us (0.903)
  waiting for transfers between devices: 150 us -> 107 us
  local copies, waits for them, and re-layouts: 63.5 us -> 68.2 us
    all_gather x2 -> x1, waiting for transfers between devices: 102 us -> 59.4 us  [softmax_heads(): lax.all_gather(jnp.concatenate([k_soft, v_soft], axis=1), 'seq', axis=0,...]
    split x0 -> x1, local copies, waits for them, and re-layouts: none -> 4.47 us  [softmax_heads(): jnp.split(lax.all_gather(jnp.concatenate([k_soft, v_soft], axis=1), 'seq'...]
  transfers between devices with their start and end apart: 5 -> 4, of which waited for: 4 -> 3; matrix products, arithmetic and copies ran while one was open for 22% -> 26% of each run, Pallas kernels for 0% -> 0%
where the time goes in v1:
time: 355 us; the launch traced here: 351 us
  waiting for transfers between devices  107 us (30%)
  loops' own time  89 us (25%)
  local copies, waits for them, and re-layouts  68.2 us (19%)
  blocking collectives  43.8 us (12%)
  other arithmetic  18.6 us (5%)
  between operations  14.7 us (4%)
  matrix products  9.85 us (3%)
    another operation x1, loops' own time, softmax_heads(): carry, _ = lax.scan(inner, carry, (key_blocks, value_blocks, firsts))  85.5 us
    all_gather x1, waiting for transfers between devices, softmax_heads(): lax.all_gather(jnp.concatenate([k_soft, v_soft], axis=1), 'seq', axis=0,...  59.4 us
    dynamic_slice x128, local copies, waits for them, and re-layouts, softmax_heads(): carry, _ = lax.scan(inner, carry, (key_blocks, value_blocks, firsts))  50.6 us
    unnamed x1, blocking collectives  43.8 us
    reduce_scatter x1, waiting for transfers between devices, local(): lax.psum_scatter(soft_term.astype(jnp.bfloat16).astype(jnp.float32).astyp...  38.3 us
    select_n x16, other arithmetic, turn(): return jax.tree.map(lambda a, b: jnp.where(reached, a, b), new, before)  14.9 us
    all_gather x1, waiting for transfers between devices, prefix(): lax.all_gather(part.astype(kind), axis)  9.04 us
  transfers between devices with their start and end apart: 4, of which 3 were waited for; matrix products, arithmetic and copies ran while one was open for 26% of the time, Pallas kernels for 0%

profile of v1, /device:TPU:0, one launch (start us, length us, event | category | flops | bytes accessed | tf_op | source)
XLA Modules:
  0.0 351.0 jit_solution(7655627925973001746)
XLA Ops:
  9.4 1.0 copy.69
  10.4 1.8 convolution_convert_fusion.2
  12.2 1.7 pad_maximum_fusion
  14.0 1.3 dynamic-slice
  16.3 43.8 %all-reduce = bf16[32]{0:T(256)(128)(2,1)S(1)} all-reduce(bf16[32]{0:T(256)(128)(2,1)S(1)} %dynamic-update-slice), channel_id=2, replica_groups=mesh['seq'=16,'head'=2] {'seq'}, use_global_device_ids=true, to_apply=%add | all-reduce | flops 32 | bytes 128
  61.4 9.0 %all-gather.7.cloned.1.call-done = bf16[32,128,128]{2,1,0:T(8,128)(2,1)} async-done(((bf16[2,128,128]{2,1,0:T(8,128)(2,1)}), bf16[32,128,128]{2,1,0:T(8,128)(2,1)}) %all-gather.7.cloned.1.call-update) | async-done | bytes 1048592 | tf_op jit(solution)/shard_map/all_gather | solution.py:14
  70.5 15.6 %while.39 = (s32[]{:T(128)}, f32[2,128,128]{2,1,0:T(8,128)S(1)}, s32[]{:T(128)}, bf16[16,2]{1,0:T(8,128)(2,1)S(1)}, bf16[16,2,128,128]{3,2,1,0:T(8,128)(2,1)}, /*index=5*/s32[]{:T(128)}, s32[]{:T(128)}) while((s32[]{:T(128)}, f32[2,128,128]{2,1,0:T(8,128)S(1)}, s32[]{:T(128)}, bf16[16,2]{1,0:T(8,128)(2,1)S(1)}, ...), condition=%wide.region_3.4_spmd.clone, body=%wide.region_2.3_spmd.clone.sunk | while | flops 163846 | bytes 327813 | solution.py:31
  86.9 2.1 convolution_convert_fusion.1
  89.1 59.4 %all-gather.5.cloned.1.call-done = bf16[4096,512]{1,0:T(8,128)(2,1)} async-done(((bf16[256,512]{1,0:T(8,128)(2,1)}), bf16[4096,512]{1,0:T(8,128)(2,1)}) %all-gather.5.cloned.1.call-update) | async-done | bytes 4194320 | tf_op jit(solution)/shard_map/all_gather | solution.py:133
  148.5 4.5 %fusion.58 = (bf16[4096,256]{1,0:T(8,128)(2,1)}, bf16[4096,256]{1,0:T(8,128)(2,1)}) fusion(bf16[4096,512]{1,0:T(8,128)(2,1)} %all-gather.5.cloned.1.call-done), kind=kLoop, calls=%fused_computation.100 | loop fusion | bytes 8388608 | tf_op jit(solution)/shard_map/split | solution.py:132
  152.9 4.1 %reshape.144 = bf16[32,128,2,128]{3,2,1,0:T(2,128)(2,1)} reshape(bf16[4096,256]{1,0:T(8,128)(2,1)} %get-tuple-element.613) | data formatting | bytes 4194304 | tf_op jit(solution)/shard_map/reshape | solution.py:140
  157.0 4.0 %reshape.143 = bf16[32,128,2,128]{3,2,1,0:T(2,128)(2,1)} reshape(bf16[4096,256]{1,0:T(8,128)(2,1)} %get-tuple-element.614) | data formatting | bytes 4194304 | tf_op jit(solution)/shard_map/reshape | solution.py:139
  161.1 141.1 %while.38 = (s32[]{:T(128)}, f32[2,128]{1,0:T(2,128)S(1)}, f32[2,128]{1,0:T(2,128)S(1)}, f32[128,2,128]{2,0,1:T(8,128)S(1)}, f32[2,128]{1,0:T(2,128)S(1)}, /*ind...) while((s32[]{:T(128)}, f32[2,128]{1,0:T(2,128)S(1)}, ...), condition=%wide.region_23.24_spmd.clone.clone, body=%wide.region_6.23_spmd.clone.clone.sunk | while | flops 34162200 | bytes 2311003 | solution.py:153
  164.3 1.0 constant_dynamic-slice_fusion.3
  169.7 1.0 constant_dynamic-slice_fusion.3
  174.6 1.0 constant_dynamic-slice_fusion.3
  179.0 1.0 constant_dynamic-slice_fusion.3
  183.3 1.0 constant_dynamic-slice_fusion.3
  187.7 1.0 constant_dynamic-slice_fusion.3
  192.1 1.0 constant_dynamic-slice_fusion.3
  196.4 1.0 constant_dynamic-slice_fusion.3
  200.8 1.0 constant_dynamic-slice_fusion.3
  205.1 1.0 constant_dynamic-slice_fusion.3
  209.5 1.0 constant_dynamic-slice_fusion.3
  213.9 1.0 constant_dynamic-slice_fusion.3
  218.2 1.0 constant_dynamic-slice_fusion.3
  222.6 1.0 constant_dynamic-slice_fusion.3
  226.9 1.0 constant_dynamic-slice_fusion.3
  231.3 1.0 constant_dynamic-slice_fusion.3
  235.7 1.0 constant_dynamic-slice_fusion.3
  302.5 3.7 %convolution_convert_fusion = bf16[256,4096]{1,0:T(8,128)(2,1)} fusion(bf16[256,4096]{1,0:T(8,128)(2,1)} %param.29, bf16[128,256]{0,1:T(8,128)(2,1)S(1)} %bitcast.150, bf16[128,256]{0,1:T(8,128)(2,1)S(1)} %bitcast.151), kind=kOutput, calls=%fused_computation.59 | convolution fusion | flops 538181632 | bytes 4325376 | tf_op jit(solution)/shard_map/dot_general | solution.py:168
  306.2 38.3 %reduce-scatter.5.cloned.1.call-done = bf16[256,2048]{1,0:T(8,128)(2,1)} async-done(((bf16[256,4096]{1,0:T(8,128)(2,1)}), bf16[256,2048]{1,0:T(8,128)(2,1)}) %reduce-scatter.5.cloned.1.call-update) | async-done | bytes 1048592 | tf_op jit(solution)/shard_map/reduce_scatter | solution.py:176
  (368 shorter events, 62.5 us)
Async XLA Ops:
  7.2 79.8 %copy-start = (bf16[256,4096]{1,0:T(8,128)(2,1)S(1)}, bf16[256,4096]{1,0:T(8,128)(2,1)}, u32[]{:S(2)}) copy-start(bf16[256,4096]{1,0:T(8,128)(2,1)} %param.28) | copy-start | bytes 6291460
  7.2 54.0 %copy-start.2 = (bf16[256,256]{1,0:T(8,128)(2,1)S(1)}, bf16[256,256]{1,0:T(8,128)(2,1)}, u32[]{:S(2)}) copy-start(bf16[256,256]{1,0:T(8,128)(2,1)} %param.21) | copy-start | bytes 393220
  7.2 63.3 %all-gather.7.cloned.1.call-start = ((), (), s32[]{:S(2)}) async-start(), calls=%async_computation.5 | async-start | bytes 1114112 | tf_op jit(solution)/shard_map/all_gather | solution.py:14
  12.2 136.3 %all-gather.5.cloned.1.call-start = ((), (), s32[]{:S(2)}) async-start(), calls=%async_computation.3 | async-start | bytes 4456448 | tf_op jit(solution)/shard_map/all_gather | solution.py:133
  13.9 72.5 %copy-start.1 = (bf16[256,256]{1,0:T(8,128)(2,1)S(1)}, bf16[256,256]{1,0:T(8,128)(2,1)}, u32[]{:S(2)}) copy-start(bf16[256,256]{1,0:T(8,128)(2,1)} %param.23) | copy-start | bytes 393220
  14.0 292.2 %reduce-scatter.3.cloned.1.call-start = ((), (), s32[]{:S(2)}) async-start(), calls=%async_computation.2 | async-start | bytes 3145728 | tf_op jit(solution)/shard_map/reduce_scatter | solution.py:170
  89.0 255.5 %reduce-scatter.5.cloned.1.call-start = ((), (), s32[]{:S(2)}) async-start(), calls=%async_computation.4 | async-start | bytes 3145728 | tf_op jit(solution)/shard_map/reduce_scatter | solution.py:176
Sparse Core Ops, SparseCore 0:
  12.3 58.1 all-gather.6
  73.8 74.6 all-gather.4
  151.3 8.2 reduce-scatter.2
  306.3 38.1 reduce-scatter.4
